TPU v7x, 32 devices: a whole 2x2x4 slice. The times are simulated.
32 devices in a mesh: rows: 8 (over z, y), tgt: 4 (over x, core).
Axes of the slice: x: 2, y: 2, z: 4, core: 2. Of those that a mesh axis runs over, the one named last changes fastest.
Arguments:
- frames: bfloat16 [16384, 512], P('rows', 'tgt'), may hold values from -6 to 6
- weights: bfloat16 [512, 1024], replicated, may hold values from -0.25 to 0.25
- phases: float32 [1024], replicated, may hold values from -3.140625 to 3.140625
- residual: float32 [16384, 1024], P('rows', 'tgt'), may hold values from -6 to 6
Outputs:
- residual_next: float32 [16384, 1024], P('rows', 'tgt')
- coefficients: float32 [1024, 1024], P(None, 'tgt')
All inputs are finite; a program needn't handle non-finite values.
Results may differ from a plain program's by a relative error of at most 0.0003.
Values may be sent and summed in bfloat16 or wider, within the bound.
A program may use at most 128 MiB of HBM per device.

v0:
```python
import jax
import jax.numpy as jnp
from jax import lax
from jax.sharding import PartitionSpec as P


def gram_of(row_block):
    return jnp.dot(
        row_block.T, row_block, precision=lax.Precision.HIGHEST, preferred_element_type=jnp.float32
    )


def body(frames, weights, phases, residual):
    highest = lax.Precision.HIGHEST
    rows_here = frames.shape[0]
    feature_count = weights.shape[1]
    preact = jnp.dot(
        lax.all_gather(frames, "tgt", axis=1, tiled=True),
        weights,
        preferred_element_type=jnp.float32,
    )
    feature = jnp.sqrt(2.0 / feature_count) * jnp.cos(preact + phases[None, :])
    quarter_rows = rows_here // lax.axis_size("tgt")
    row_block = lax.dynamic_slice_in_dim(
        feature, lax.axis_index("tgt") * quarter_rows, quarter_rows, 0
    )
    gram_matrix = lax.psum(gram_of(row_block), ("rows", "tgt"))
    total_rows = rows_here * lax.axis_size("rows")
    gram_matrix = gram_matrix + 0.1 * total_rows / feature_count * jnp.eye(
        feature_count, dtype=jnp.float32
    )
    factor = jnp.linalg.cholesky(gram_matrix)
    correlation = jnp.dot(
        feature.T, residual, precision=highest, preferred_element_type=jnp.float32
    )
    correlation = lax.psum(correlation, "rows")
    coefficients = jax.scipy.linalg.cho_solve((factor, True), correlation)
    residual_next = residual - jnp.dot(
        feature, coefficients, precision=highest, preferred_element_type=jnp.float32
    )
    return (residual_next, coefficients)


def solution(mesh):
    return jax.shard_map(
        body,
        mesh=mesh,
        in_specs=(P("rows", "tgt"), P(), P(), P("rows", "tgt")),
        out_specs=(P("rows", "tgt"), P(None, "tgt")),
        check_vma=False,
    )
```

profile of v0, /device:TPU:0, one launch (start us, length us, event | category | flops | bytes accessed | tf_op | source)
XLA Modules:
  0.0 615.2 jit_solution(7062318444680605771)
XLA Ops:
  8.0 27.2 %all-gather.2.cloned.1.call-done = bf16[2048,512]{1,0:T(8,128)(2,1)} async-done(((bf16[2048,128]{1,0:T(8,128)(2,1)}), bf16[2048,512]{1,0:T(8,128)(2,1)}) %all-gather.2.cloned.1.call-update) | async-done | bytes 2097168 | tf_op jit(solution)/shard_map/all_gather | solution.py:18
  35.1 29.7 %cosine_multiply_fusion = f32[2048,1024]{1,0:T(8,128)S(1)} fusion(f32[1024]{0:T(1024)} %param.6, bf16[2048,512]{1,0:T(8,128)(2,1)} %all-gather.2.cloned.1.call-done, bf16[512,1024]{1,0:T(8,128)(2,1)S(1)} %copy-done), kind=kOutput, calls=%fused_computation.2 | convolution fusion | flops 2151677952 | bytes 11538432 | tf_op jit(solution)/shard_map/dot_general | solution.py:17
  64.9 3.2 copy-done.1
  68.1 8.5 %fusion.1 = f32[1024,1024]{0,1:T(8,128)} fusion(f32[2048,1024]{1,0:T(8,128)S(1)} %cosine_multiply_fusion, s32[]{:T(128)S(6)} %select_n.7), kind=kOutput, calls=%fused_computation.10 | convolution fusion | flops 6442450944 | bytes 6291460 | tf_op jit(solution)/shard_map/dot_general | solution.py:8
  77.4 16.3 %fusion.98 = f32[1024,256]{1,0:T(8,128)} fusion(f32[2048,1024]{1,0:T(8,128)} %copy-done.1, f32[2048,256]{1,0:T(8,128)S(1)} %copy-done.3), kind=kOutput, calls=%fused_computation.220 | convolution fusion | flops 6442450944 | bytes 11534336 | tf_op jit(solution)/shard_map/dot_general | solution.py:33
  93.8 124.8 %all-reduce.4.cloned.1.call-done = f32[1024,1024]{0,1:T(8,128)} async-done(((f32[1024,1024]{0,1:T(8,128)}), f32[1024,1024]{0,1:T(8,128)}) %all-reduce.4.cloned.1.call-update) | async-done | bytes 4194320 | tf_op jit(solution)/shard_map/psum | solution.py:27
  218.6 4.8 select_add_fusion
  223.4 5.8 copy.7
  229.2 4.5 fusion
  233.6 2.0 copy-done.5
  235.6 11.7 %cholesky.222 = f32[128,128]{1,0:T(8,128)S(1)} custom-call(f32[128,128]{1,0:T(8,128)S(1)} %cholesky.577), custom_call_target="Cholesky" | custom-call | tf_op jit(solution)/shard_map/jit(cholesky)/cholesky | solution.py:32
  247.4 9.8 %custom-call.66 = f32[1,128,128]{1,2,0:T(8,128)S(1)} custom-call(f32[1,128,128]{2,1,0:T(8,128)S(1)} %get-tuple-element.54), custom_call_target="InvertDiagBlocksLowerTriangular" | custom-call | tf_op jit(solution)/shard_map/jit(cholesky)/cholesky | solution.py:32
  257.2 1.5 fusion.25
  259.5 1.6 convolution_subtract_fusion.1
  261.9 11.7 %cholesky.243 = f32[128,128]{1,0:T(8,128)S(1)} custom-call(f32[128,128]{1,0:T(8,128)S(1)} %cholesky.581), custom_call_target="Cholesky" | custom-call | tf_op jit(solution)/shard_map/jit(cholesky)/cholesky | solution.py:32
  273.7 2.2 copy.9
  276.0 9.8 %custom-call.67 = f32[1,128,128]{1,2,0:T(8,128)S(1)} custom-call(f32[1,128,128]{2,1,0:T(8,128)S(1)} %get-tuple-element.52), custom_call_target="InvertDiagBlocksLowerTriangular" | custom-call | tf_op jit(solution)/shard_map/jit(cholesky)/cholesky | solution.py:32
  287.6 1.9 copy-done.2
  289.5 2.4 convolution_subtract_fusion.2
  292.5 13.2 %cholesky.466 = f32[128,128]{1,0:T(8,128)} custom-call(f32[128,128]{1,0:T(8,128)} %cholesky.586), custom_call_target="Cholesky" | custom-call | tf_op jit(solution)/shard_map/jit(cholesky)/cholesky | solution.py:32
  305.7 1.5 select_reduce_fusion.5
  307.2 1.6 copy.12
  308.7 1.5 constant_dynamic-update-slice_fusion.46
  310.2 11.3 %custom-call.68 = f32[1,128,128]{1,2,0:T(8,128)} custom-call(f32[1,128,128]{2,1,0:T(8,128)} %get-tuple-element.50), custom_call_target="InvertDiagBlocksLowerTriangular" | custom-call | tf_op jit(solution)/shard_map/jit(cholesky)/cholesky | solution.py:32
  321.5 2.1 convolution_dynamic-update-slice_fusion.1
  323.6 3.3 convolution_subtract_fusion.3
  327.5 12.5 %cholesky.485 = f32[128,128]{1,0:T(8,128)S(1)} custom-call(f32[128,128]{1,0:T(8,128)} %cholesky.591), custom_call_target="Cholesky" | custom-call | tf_op jit(solution)/shard_map/jit(cholesky)/cholesky | solution.py:32
  341.4 1.5 constant_dynamic-update-slice_fusion.45
  342.9 10.6 %custom-call.69 = f32[1,128,128]{1,2,0:T(8,128)S(1)} custom-call(f32[1,128,128]{2,1,0:T(8,128)} %get-tuple-element.48), custom_call_target="InvertDiagBlocksLowerTriangular" | custom-call | tf_op jit(solution)/shard_map/jit(cholesky)/cholesky | solution.py:32
  354.7 3.2 convolution_subtract_fusion.4
  357.9 12.1 %cholesky.504 = f32[128,128]{1,0:T(8,128)S(1)} custom-call(f32[128,128]{1,0:T(8,128)S(1)} %cholesky.596), custom_call_target="Cholesky" | custom-call | tf_op jit(solution)/shard_map/jit(cholesky)/cholesky | solution.py:32
  370.0 1.2 select_reduce_fusion.3
  371.9 10.6 %custom-call.70 = f32[1,128,128]{1,2,0:T(8,128)S(1)} custom-call(f32[1,128,128]{2,1,0:T(8,128)} %get-tuple-element.46), custom_call_target="InvertDiagBlocksLowerTriangular" | custom-call | tf_op jit(solution)/shard_map/jit(cholesky)/cholesky | solution.py:32
  383.7 3.1 convolution_subtract_fusion.5
  386.8 11.7 %cholesky.524 = f32[128,128]{1,0:T(8,128)S(1)} custom-call(f32[128,128]{1,0:T(8,128)S(1)} %cholesky.601), custom_call_target="Cholesky" | custom-call | tf_op jit(solution)/shard_map/jit(cholesky)/cholesky | solution.py:32
  399.8 9.8 %custom-call.71 = f32[1,128,128]{1,2,0:T(8,128)S(1)} custom-call(f32[1,128,128]{2,1,0:T(8,128)S(1)} %get-tuple-element.44), custom_call_target="InvertDiagBlocksLowerTriangular" | custom-call | tf_op jit(solution)/shard_map/jit(cholesky)/cholesky | solution.py:32
  410.6 2.8 convolution_subtract_fusion.18
  413.4 11.7 %cholesky.544 = f32[128,128]{1,0:T(8,128)S(1)} custom-call(f32[128,128]{1,0:T(8,128)S(1)} %cholesky.606), custom_call_target="Cholesky" | custom-call | tf_op jit(solution)/shard_map/jit(cholesky)/cholesky | solution.py:32
  425.9 9.8 %custom-call.72 = f32[1,128,128]{1,2,0:T(8,128)S(1)} custom-call(f32[1,128,128]{2,1,0:T(8,128)S(1)} %get-tuple-element.42), custom_call_target="InvertDiagBlocksLowerTriangular" | custom-call | tf_op jit(solution)/shard_map/jit(cholesky)/cholesky | solution.py:32
  436.7 2.1 convolution_subtract_fusion.21
  438.8 11.7 %cholesky.562 = f32[128,128]{1,0:T(8,128)S(1)} custom-call(f32[128,128]{1,0:T(8,128)S(1)} %convolution_subtract_fusion.21), custom_call_target="Cholesky" | custom-call | tf_op jit(solution)/shard_map/jit(cholesky)/cholesky | solution.py:32
  452.0 1.3 compare_reduce_fusion.3
  453.3 1.2 compare_reduce_fusion.2
  462.1 4.9 select_select_fusion
  467.0 29.3 %while.1 = (s32[]{:T(128)}, f32[1024,1024]{0,1:T(8,128)}, s32[8,2]{0,1:T(2,128)S(1)}, f32[8,128,128]{2,1,0:T(8,128)}, s32[]{:T(128)}) while((s32[]{:T(128)}, f32[1024,1024]{0,1:T(8,128)}, s32[8,2]{0,1:T(2,128)S(1)}, f32[8,128,128]{2,1,0:T(8,128)}, s32[]{:T(128)}) %tuple.53), condition=%wide.while_cond, body=%wide.while_body.sunk | while | flops 2 | bytes 393829 | solution.py:37
  467.7 2.3 dynamic-slice.7
  471.3 2.3 dynamic-slice.7
  475.0 2.3 dynamic-slice.7
  478.7 2.3 dynamic-slice.7
  482.4 2.3 dynamic-slice.7
  486.0 2.3 dynamic-slice.7
  489.7 2.3 dynamic-slice.7
  493.4 2.2 dynamic-slice.7
  496.3 80.2 %custom-call.73 = f32[8,128,128]{1,2,0:T(8,128)} custom-call(f32[8,128,128]{2,1,0:T(8,128)} %get-tuple-element.9), custom_call_target="InvertDiagBlocksLowerTriangular" | custom-call | tf_op jit(solution)/shard_map/jit(_cho_solve)/triangular_solve | solution.py:37
  576.6 1.4 constant_dynamic-update-slice_fusion.10
  578.0 1.3 convolution_subtract_fusion.17
  580.5 1.4 convolution_subtract_fusion.13
  581.9 1.2 constant_dynamic-update-slice_fusion.8
  583.0 1.5 convolution_subtract_fusion.12
  585.7 1.5 convolution_subtract_fusion.11
  587.6 1.6 convolution_subtract_fusion.10
  589.6 1.8 convolution_subtract_fusion.16
  591.6 1.9 convolution_subtract_fusion.20
  599.7 8.5 %convolution_subtract_fusion = f32[2048,256]{1,0:T(8,128)} fusion(f32[2048,256]{1,0:T(8,128)S(1)} %copy-done.3, f32[2048,1024]{1,0:T(8,128)S(1)} %bitcast.132, f32[1024,256]{1,0:T(8,128)S(1)} %constant_dynamic-update-slice_fusion.36), kind=kOutput, calls=%fused_computation.9 | convolution fusion | flops 6442975232 | bytes 13631488 | tf_op jit(solution)/shard_map/dot_general | solution.py:38
  (150 shorter events, 39.0 us)
Async XLA Ops:
  7.2 28.0 %copy-start = (bf16[512,1024]{1,0:T(8,128)(2,1)S(1)}, bf16[512,1024]{1,0:T(8,128)(2,1)}, u32[]{:S(2)}) copy-start(bf16[512,1024]{1,0:T(8,128)(2,1)} %param.5) | copy-start | bytes 3145732
  7.2 28.0 %all-gather.2.cloned.1.call-start = ((), (), s32[]{:S(2)}) async-start(), calls=%async_computation | async-start | bytes 2621440 | tf_op jit(solution)/shard_map/all_gather | solution.py:18
  7.9 210.7 %all-reduce.4.cloned.1.call-start = ((), (), s32[]{:S(2)}) async-start(), calls=%async_computation.1 | async-start | bytes 8388608 | tf_op jit(solution)/shard_map/psum | solution.py:27
  64.9 3.2 copy-start.1
  68.1 9.3 %copy-start.3 = (f32[2048,256]{1,0:T(8,128)S(1)}, f32[2048,256]{1,0:T(8,128)}, u32[]{:S(2)}) copy-start(f32[2048,256]{1,0:T(8,128)} %param.7) | copy-start | bytes 6291460
  76.6 499.9 %all-reduce.6.cloned.1.call-start = ((), (), s32[]{:S(2)}) async-start(), calls=%async_computation.2 | async-start | bytes 2097152 | tf_op jit(solution)/shard_map/psum | solution.py:36
  233.6 2.0 copy-start.5
  258.7 0.8 copy-start.6
  261.1 0.8 copy-start.9
  285.8 1.0 copy-start.8
  285.8 1.2 copy-start.10
  287.5 2.0 copy-start.2
  462.1 4.9 copy-start.12
  576.6 9.1 %copy-start.4 = (f32[1024,1024]{0,1:T(8,128)S(1)}, f32[1024,1024]{0,1:T(8,128)}, u32[]{:S(2)}) copy-start(f32[1024,1024]{0,1:T(8,128)} %get-tuple-element.119) | copy-start | bytes 12582916
  576.6 10.7 %copy-start.7 = (f32[8,128,128]{1,2,0:T(8,128)S(1)}, f32[8,128,128]{1,2,0:T(8,128)}, u32[]{:S(2)}) copy-start(f32[8,128,128]{1,2,0:T(8,128)} %custom-call.73) | copy-start | bytes 1572868
  594.4 5.1 slice-start
  597.5 2.2 slice-start.1
  599.7 8.5 %copy-start.11 = (f32[1024,256]{1,0:T(8,128)}, f32[1024,256]{1,0:T(8,128)S(1)}, u32[]{:S(2)}) copy-start(f32[1024,256]{1,0:T(8,128)S(1)} %constant_dynamic-update-slice_fusion.36) | copy-start | bytes 3145732
Sparse Core Ops, SparseCore 0:
  9.6 25.5 all-gather.1
  76.8 141.7 all-reduce.3
  222.7 77.5 all-reduce.5
where the time goes:
time: 625 us; the launch traced here: 615 us
  other arithmetic  273 us (44%)
  waiting for transfers between devices  153 us (24%)
  matrix products  112 us (18%)
  local copies, waits for them, and re-layouts  57.2 us (9%)
  between operations  20 us (3%)
    another operation x30, other arithmetic, body(): factor = jnp.linalg.cholesky(gram_matrix)  178 us
    psum x1, waiting for transfers between devices, body(): gram_matrix = lax.psum(gram_of(row_block), ('rows', 'tgt'))  125 us
    another operation x3, other arithmetic, body(): coefficients = jax.scipy.linalg.cho_solve((factor, True), correlation)  85.6 us
    dot_general x1, matrix products, body(): jnp.dot(lax.all_gather(frames, 'tgt', axis=1, tiled=True), weights, prefe...  29.7 us
    another operation x40, local copies, waits for them, and re-layouts  29.2 us
    all_gather x1, waiting for transfers between devices, body(): lax.all_gather(frames, 'tgt', axis=1, tiled=True)  27.2 us
    another operation x14, matrix products, body(): factor = jnp.linalg.cholesky(gram_matrix)  26.7 us
    another operation x30, matrix products, body(): coefficients = jax.scipy.linalg.cho_solve((factor, True), correlation)  22.2 us
  transfers between devices with their start and end apart: 3, of which 2 were waited for; matrix products, arithmetic and copies ran while one was open for 59% of the time, Pallas kernels for 0%

commit v1 on v0

v1 whole, which is shorter than its diff:
```python
import functools
import math

import jax
import jax.numpy as jnp
from jax import lax
from jax.experimental import pallas as pl
from jax.experimental.pallas import tpu as pltpu
from jax.sharding import PartitionSpec as P

HIGHEST = lax.Precision.HIGHEST
PANEL = 128
LIMIT = 48 * 1024 * 1024
HALF = (
    0.9999999997778334,
    -0.49999999352232993 / 4,
    0.04166663603866973 / 16,
    -0.001388835871629621 / 64,
    2.4760028045058155e-05 / 256,
    -2.604918848612031e-07 / 1024,
)


def cosine(angle):
    turns = jnp.round(angle * (1.0 / (2.0 * math.pi)))
    rest = (angle - turns * 6.28125) - turns * (2.0 * math.pi - 6.28125)
    square = rest * rest
    half = jnp.full_like(square, HALF[-1])
    for term in HALF[-2::-1]:
        half = half * square + term
    return 2.0 * half * half - 1.0


def dot(a, b):
    return jnp.dot(a, b, precision=HIGHEST, preferred_element_type=jnp.float32)


def inverse(tiles):
    lanes = tiles[0].shape[1]
    lane = lax.broadcasted_iota(jnp.int32, (8, lanes), 1)
    sub = lax.broadcasted_iota(jnp.int32, (8, lanes), 0)
    for k in range(0, lanes, 2):
        own, at = divmod(k, 8)
        first = lane == k
        second = lane == k + 1
        either = first | second
        col0 = [jnp.broadcast_to(t[:, k:k + 1], t.shape) for t in tiles]
        col1 = [jnp.broadcast_to(t[:, k + 1:k + 2], t.shape) for t in tiles]

        def spread(tile, row):
            return jnp.broadcast_to(tile[row:row + 1, :], tile.shape)

        a = spread(col0[own], at)
        b = spread(col1[own], at)
        d = spread(col1[own], at + 1)
        row0 = spread(tiles[own], at)
        row1 = spread(tiles[own], at + 1)
        row0 = jnp.where(first, 1.0, jnp.where(second, 0.0, row0))
        row1 = jnp.where(second, 1.0, jnp.where(first, 0.0, row1))
        scale = 1.0 / (a * d - b * b)
        t0 = (d * row0 - b * row1) * scale
        t1 = (a * row1 - b * row0) * scale
        out = []
        for i, tile in enumerate(tiles):
            new = jnp.where(either, 0.0, tile) - col0[i] * t0 - col1[i] * t1
            if i == own:
                new = jnp.where(sub == at, t0, jnp.where(sub == at + 1, t1, new))
            out.append(new)
        tiles = out
    return tiles


def factor_kernel(ridge, gram_ref, work_ref, inv_ref):
    size = gram_ref.shape[0]
    panels = size // PANEL
    diag = lax.broadcasted_iota(jnp.int32, (PANEL, size), 0)
    lane = lax.broadcasted_iota(jnp.int32, (PANEL, size), 1)

    @pl.loop(0, panels)
    def _(p):
        rows = pl.ds(pl.multiple_of(p * PANEL, PANEL), PANEL)
        work_ref[rows, :] = gram_ref[rows, :] + jnp.where(lane == diag + p * PANEL, ridge, 0.0)

    @pl.loop(0, panels)
    def _(p):
        start = pl.multiple_of(p * PANEL, PANEL)
        rows = pl.ds(start, PANEL)
        tiles = [work_ref[pl.ds(start + 8 * i, 8), rows] for i in range(PANEL // 8)]
        tiles = inverse(tiles)
        for i, tile in enumerate(tiles):
            inv_ref[pl.ds(start + 8 * i, 8), :] = tile
        right = lane >= start + PANEL
        scaled = jnp.where(right, dot(inv_ref[rows, :], work_ref[rows, :]), 0.0)
        work_ref[rows, :] = jnp.where(right, scaled, work_ref[rows, :])

        @pl.loop(p + 1, panels)
        def _(q):
            below = pl.ds(pl.multiple_of(q * PANEL, PANEL), PANEL)
            work_ref[below, :] = work_ref[below, :] - dot(work_ref[below, rows], scaled)


def solve_kernel(work_ref, inv_ref, corr_ref, out_ref):
    panels = work_ref.shape[0] // PANEL
    for p in range(panels):
        rows = slice(p * PANEL, (p + 1) * PANEL)
        here = corr_ref[rows, :]
        if p:
            here = here - dot(work_ref[rows, :p * PANEL], out_ref[:p * PANEL, :])
        out_ref[rows, :] = dot(inv_ref[rows, :], here)
    for p in range(panels - 2, -1, -1):
        rows = slice(p * PANEL, (p + 1) * PANEL)
        out_ref[rows, :] = out_ref[rows, :] - dot(
            work_ref[rows, (p + 1) * PANEL:], out_ref[(p + 1) * PANEL:, :]
        )


def body(frames, weights, phases, residual):
    rows_here = frames.shape[0]
    feature_count = weights.shape[1]
    preact = jnp.dot(
        lax.all_gather(frames, "tgt", axis=1, tiled=True),
        weights,
        preferred_element_type=jnp.float32,
    )
    feature = math.sqrt(2.0 / feature_count) * cosine(preact + phases[None, :])
    share = feature_count // lax.axis_size("tgt")
    mine = lax.dynamic_slice_in_dim(feature, lax.axis_index("tgt") * share, share, 1)
    gram = lax.psum(dot(mine.T, feature), "rows")
    corr, gram = lax.optimization_barrier((dot(feature.T, residual), gram))
    gram = lax.all_gather(gram, "tgt", axis=0, tiled=True)
    corr = lax.psum(corr, "rows")
    ridge = 0.1 * (rows_here * lax.axis_size("rows")) / feature_count
    work, inv = pl.pallas_call(
        functools.partial(factor_kernel, ridge),
        out_shape=(
            jax.ShapeDtypeStruct(gram.shape, jnp.float32),
            jax.ShapeDtypeStruct((feature_count, PANEL), jnp.float32),
        ),
        compiler_params=pltpu.CompilerParams(vmem_limit_bytes=LIMIT),
        cost_estimate=pl.CostEstimate(
            flops=8 * feature_count**3, bytes_accessed=8 * feature_count**2, transcendentals=0
        ),
        name="factor",
    )(gram)
    coefficients = pl.pallas_call(
        solve_kernel,
        out_shape=jax.ShapeDtypeStruct(corr.shape, jnp.float32),
        compiler_params=pltpu.CompilerParams(vmem_limit_bytes=LIMIT),
        name="solve",
    )(work, inv, corr)
    residual_next = residual - dot(feature, coefficients)
    return (residual_next, coefficients)


def solution(mesh):
    return jax.shard_map(
        body,
        mesh=mesh,
        in_specs=(P("rows", "tgt"), P(), P(), P("rows", "tgt")),
        out_specs=(P("rows", "tgt"), P(None, "tgt")),
        check_vma=False,
    )
```

time: 625 us -> 307 us (0.49); the launches traced: 615 us -> 306 us
  other arithmetic: 273 us -> 0 us
  Pallas kernels: 0 us -> 114 us
  matrix products: 112 us -> 43.9 us
  local copies, waits for them, and re-layouts: 57.2 us -> 8.6 us
  waiting for transfers between devices: 153 us -> 125 us
    another operation x33 -> x0, other arithmetic: 264 us -> none  [the longest x30 178 us: body(): factor = jnp.linalg.cholesky(gram_matrix)]
    pallas_call x0 -> x2, Pallas kernels: none -> 114 us  [the longest x1 103 us: body(): pl.pallas_call(functools.partial(factor_kernel, ridge), out_shape=(jax.Sh...]
    psum x2, waiting for transfers between devices: 125 us -> 61.7 us  [the longest x1 61.7 us: body(): gram = lax.psum(dot(mine.T, feature), 'rows')]
    another operation x44 -> x0, matrix products: 48.9 us -> none  [the longest x14 26.7 us: body(): factor = jnp.linalg.cholesky(gram_matrix)]
    another operation x70 -> x0, local copies, waits for them, and re-layouts: 41.6 us -> none
    all_gather x0 -> x1, waiting for transfers between devices: none -> 35.1 us  [body(): gram = lax.all_gather(gram, 'tgt', axis=0, tiled=True)]
    dot_general x1, matrix products: 29.7 us -> 8.97 us  [body(): jnp.dot(lax.all_gather(frames, 'tgt', axis=1, tiled=True), weights, prefe...]
  transfers between devices with their start and end apart: 3 -> 4, of which waited for: 2 -> 3; matrix products, arithmetic and copies ran while one was open for 59% -> 5% of each run, Pallas kernels for 0% -> 34%
where the time goes in v1:
time: 307 us; the launch traced here: 306 us
  waiting for transfers between devices  125 us (41%)
  Pallas kernels  114 us (37%)
  matrix products  43.9 us (14%)
  between operations  13.8 us (4%)
  local copies, waits for them, and re-layouts  8.6 us (3%)
    pallas_call x1, Pallas kernels, body(): pl.pallas_call(functools.partial(factor_kernel, ridge), out_shape=(jax.Sh...  103 us
    psum x1, waiting for transfers between devices, body(): gram = lax.psum(dot(mine.T, feature), 'rows')  61.7 us
    all_gather x1, waiting for transfers between devices, body(): gram = lax.all_gather(gram, 'tgt', axis=0, tiled=True)  35.1 us
    dot_general x3, matrix products, dot(): return jnp.dot(a, b, precision=HIGHEST, preferred_element_type=jnp.float32)  34.9 us
    all_gather x1, waiting for transfers between devices, body(): lax.all_gather(frames, 'tgt', axis=1, tiled=True)  27.2 us
    pallas_call x1, Pallas kernels, body(): pl.pallas_call(solve_kernel, out_shape=jax.ShapeDtypeStruct(corr.shape, j...  11.4 us
    dot_general x1, matrix products, body(): jnp.dot(lax.all_gather(frames, 'tgt', axis=1, tiled=True), weights, prefe...  8.97 us
    unnamed x14, local copies, waits for them, and re-layouts  8.6 us
  transfers between devices with their start and end apart: 4, of which 3 were waited for; matrix products, arithmetic and copies ran while one was open for 5% of the time, Pallas kernels for 34%

profile of v1, /device:TPU:0, one launch (start us, length us, event | category | flops | bytes accessed | tf_op | source)
XLA Modules:
  0.0 306.3 jit_solution(17534858938472832301)
XLA Ops:
  7.2 0.0 copy-start
  7.2 0.0 all-gather.3.cloned.1.call-start
  7.2 0.7 all-gather.3.cloned.1.call-update
  7.9 0.0 all-reduce.3.cloned.1.call-start
  8.0 27.2 %all-gather.3.cloned.1.call-done = bf16[2048,512]{1,0:T(8,128)(2,1)} async-done(((bf16[2048,128]{1,0:T(8,128)(2,1)}), bf16[2048,512]{1,0:T(8,128)(2,1)}) %all-gather.3.cloned.1.call-update) | async-done | bytes 2097168 | tf_op jit(solution)/shard_map/all_gather | solution.py:121
  35.1 0.0 copy-done
  35.1 9.0 %fusion.1 = f32[2048,1024]{1,0:T(8,128)S(1)} fusion(f32[1024]{0:T(1024)} %param.6, bf16[2048,512]{1,0:T(8,128)(2,1)} %all-gather.3.cloned.1.call-done, bf16[512,1024]{1,0:T(8,128)(2,1)S(1)} %copy-done), kind=kOutput, calls=%fused_computation.2 | convolution fusion | flops 2193620992 | bytes 11538432 | tf_op jit(solution)/shard_map/dot_general | solution.py:120
  44.1 0.0 copy-start.4
  44.1 3.2 %copy-done.4 = f32[2048,1024]{1,0:T(8,128)} copy-done((f32[2048,1024]{1,0:T(8,128)}, f32[2048,1024]{1,0:T(8,128)S(1)}, u32[]{:S(2)}) %copy-start.4) | copy-done | bytes 8388632
  47.3 0.0 copy-start.5
  47.3 8.3 %fusion.2 = f32[256,1024]{1,0:T(8,128)} fusion(f32[2048,1024]{1,0:T(8,128)S(1)} %fusion.1, s32[]{:T(128)S(6)} %select_n.3), kind=kOutput, calls=%fused_computation.4 | convolution fusion | flops 6442450944 | bytes 11534340 | tf_op jit(solution)/shard_map/dot_general | solution.py:35
  55.6 0.0 all-reduce.3.cloned.1.call-update
  55.6 0.2 all-gather.5.cloned.1.call-start
  55.9 0.0 copy-done.5
  55.9 16.3 %fusion.5 = f32[1024,256]{1,0:T(8,128)} fusion(f32[2048,1024]{1,0:T(8,128)} %copy-done.4, f32[2048,256]{1,0:T(8,128)S(1)} %copy-done.5), kind=kOutput, calls=%fused_computation.7 | convolution fusion | flops 6442450944 | bytes 11534336 | tf_op jit(solution)/shard_map/dot_general | solution.py:35
  72.2 61.7 %all-reduce.3.cloned.1.call-done = f32[256,1024]{1,0:T(8,128)} async-done(((f32[256,1024]{1,0:T(8,128)}), f32[256,1024]{1,0:T(8,128)}) %all-reduce.3.cloned.1.call-update) | async-done | bytes 1048592 | tf_op jit(solution)/shard_map/psum | solution.py:128
  133.9 0.0 all-gather.5.cloned.1.call-update
  133.9 0.0 all-reduce.5.cloned.1.call-start
  134.0 0.5 all-reduce.5.cloned.1.call-update
  134.5 35.1 %all-gather.5.cloned.1.call-done.gram_ref = f32[1024,1024]{1,0:T(8,128)} async-done(((f32[256,1024]{1,0:T(8,128)}), f32[1024,1024]{1,0:T(8,128)}) %all-gather.5.cloned.1.call-update) | async-done | bytes 4194320 | tf_op jit(solution)/shard_map/all_gather | solution.py:130
  169.7 103.0 %factor.1 = (f32[1024,1024]{1,0:T(8,128)S(1)}, f32[1024,128]{1,0:T(8,128)S(1)}) custom-call(f32[1024,1024]{1,0:T(8,128)} %all-gather.5.cloned.1.call-done.gram_ref), custom_call_target="tpu_custom_call" | custom-call | flops 8589934592 | bytes 8388608 | tf_op jit(solution)/shard_map/factor/pallas_call | solution.py:133
  272.7 0.0 copy-start.1
  272.7 2.0 copy-done.1
  274.7 0.0 all-reduce.5.cloned.1.call-done.corr_ref
  274.7 0.0 copy-start.2
  274.7 2.2 copy-done.2
  276.8 0.0 copy-start.3
  276.8 1.2 copy-done.3
  278.1 0.0 copy-start.6
  278.1 11.4 %solve.1 = f32[1024,256]{1,0:T(8,128)} custom-call(f32[1024,1024]{1,0:T(8,128)S(1)} %copy-done.2, f32[1024,128]{1,0:T(8,128)S(1)} %get-tuple-element.8.inv_ref, f32[1024,256]{1,0:T(8,128)S(1)} %copy-done.3), custom_call_target="tpu_custom_call" | custom-call | tf_op jit(solution)/shard_map/solve/pallas_call | solution.py:145
  289.5 0.0 copy-done.6
  289.5 10.3 %convolution_subtract_fusion = f32[2048,256]{1,0:T(8,128)} fusion(f32[2048,256]{1,0:T(8,128)S(1)} %copy-done.6, f32[2048,1024]{1,0:T(8,128)} %copy-done.4, f32[1024,256]{1,0:T(8,128)} %solve.1), kind=kOutput, calls=%fused_computation.3 | convolution fusion | flops 6442975232 | bytes 13631488 | tf_op jit(solution)/shard_map/dot_general | solution.py:35
Async XLA Ops:
  7.2 28.0 %copy-start = (bf16[512,1024]{1,0:T(8,128)(2,1)S(1)}, bf16[512,1024]{1,0:T(8,128)(2,1)}, u32[]{:S(2)}) copy-start(bf16[512,1024]{1,0:T(8,128)(2,1)} %param.5) | copy-start | bytes 3145732
  7.2 28.0 %all-gather.3.cloned.1.call-start = ((), (), s32[]{:S(2)}) async-start(), calls=%async_computation | async-start | bytes 2621440 | tf_op jit(solution)/shard_map/all_gather | solution.py:121
  7.9 126.0 %all-reduce.3.cloned.1.call-start = ((), (), s32[]{:S(2)}) async-start(), calls=%async_computation.1 | async-start | bytes 2097152 | tf_op jit(solution)/shard_map/psum | solution.py:128
  44.1 3.2 %copy-start.4 = (f32[2048,1024]{1,0:T(8,128)}, f32[2048,1024]{1,0:T(8,128)S(1)}, u32[]{:S(2)}) copy-start(f32[2048,1024]{1,0:T(8,128)S(1)} %fusion.1) | copy-start | bytes 25165828
  47.3 8.5 %copy-start.5 = (f32[2048,256]{1,0:T(8,128)S(1)}, f32[2048,256]{1,0:T(8,128)}, u32[]{:S(2)}) copy-start(f32[2048,256]{1,0:T(8,128)} %param.7) | copy-start | bytes 6291460
  55.6 114.0 %all-gather.5.cloned.1.call-start = ((), (), s32[]{:S(2)}) async-start(), calls=%async_computation.2 | async-start | bytes 5242880 | tf_op jit(solution)/shard_map/all_gather | solution.py:130
  133.9 140.7 %all-reduce.5.cloned.1.call-start = ((), (), s32[]{:S(2)}) async-start(), calls=%async_computation.3 | async-start | bytes 2097152 | tf_op jit(solution)/shard_map/psum | solution.py:131
  272.7 2.0 copy-start.1
  274.7 2.2 copy-start.2
  276.8 1.2 copy-start.3
  278.1 11.4 %copy-start.6 = (f32[2048,256]{1,0:T(8,128)S(1)}, f32[2048,256]{1,0:T(8,128)}, u32[]{:S(2)}) copy-start(f32[2048,256]{1,0:T(8,128)} %param.7) | copy-start | bytes 6291460
Sparse Core Ops, SparseCore 0:
  9.6 25.5 all-gather.2
  55.8 78.1 all-reduce.2
  135.6 34.0 all-gather.4
  174.0 78.4 all-reduce.4
